TPU v7x, 1024 devices: a whole 4x8x16 slice. The times are simulated.
1024 devices in a mesh: gx: 16 (over x, z_lo), gy: 8 (over y), gz: 8 (over z_hi, core).
Axes of the slice: x: 4, y: 8, z: 16 (z_hi: 4, z_lo: 4; z = z_hi * 4 + z_lo), core: 2. Of those that a mesh axis runs over, the one named last changes fastest.
Arguments:
- tokens: bfloat16 [384, 6144], P(('gx', 'gy'), 'gz'), may hold values from -6 to 6
- w_up: bfloat16 [6144, 49152], P('gz', ('gx', 'gy')), may hold values from -0.078125 to 0.078125
- w_down: bfloat16 [49152, 6144], P(('gx', 'gy'), 'gz'), may hold values from -0.02734375 to 0.02734375
- cotangent: bfloat16 [384, 6144], P(('gx', 'gy'), 'gz'), may hold values from -6 to 6
Outputs:
- grad_in: float32 [384, 6144], P(('gx', 'gy'), 'gz')
- grad_up: bfloat16 [6144, 49152], P('gz', ('gx', 'gy'))
- grad_down: bfloat16 [49152, 6144], P(('gx', 'gy'), 'gz')
All inputs are finite; a program needn't handle non-finite values.
Results may differ from a plain program's by a relative error of at most 0.0049.
Values may be sent and summed in bfloat16 or wider, within the bound.
A program may use at most 32 MiB of HBM per device.

v0:
```python
import math

import jax
import jax.numpy as jnp
from jax import lax
from jax.sharding import PartitionSpec as P

GELU_SCALE = math.sqrt(2.0 / math.pi)
CUBIC_COEFF = 0.044715


def activate(pre_act, back_grad):
    squared = pre_act * pre_act
    tangent = jnp.tanh(GELU_SCALE * pre_act * (1.0 + CUBIC_COEFF * squared))
    hidden = (0.5 * pre_act * (1.0 + tangent)).astype(jnp.bfloat16)
    gelu_slope = 0.5 * (1.0 + tangent) + 0.5 * pre_act * (1.0 - tangent * tangent) * GELU_SCALE * (
        1.0 + 3.0 * CUBIC_COEFF * squared
    )
    return (hidden, (back_grad * gelu_slope).astype(jnp.bfloat16))


def on_device(tokens, w_up, w_down, cotangent):
    rows_all, cot_all = (
        lax.all_gather(tokens, ("gx", "gy"), axis=0, tiled=True),
        lax.all_gather(cotangent, ("gx", "gy"), axis=0, tiled=True),
    )
    pre_part = jnp.dot(rows_all, w_up, preferred_element_type=jnp.float32)
    back_part = jnp.einsum("td,fd->tf", cot_all, w_down, preferred_element_type=jnp.float32)
    pre_act, back_grad = lax.psum((pre_part, back_part), "gz")
    hidden, pre_grad = activate(pre_act, back_grad)
    grad_up = jnp.einsum(
        "td,tf->df", rows_all, pre_grad, preferred_element_type=jnp.float32
    ).astype(jnp.bfloat16)
    grad_down = jnp.einsum("tf,td->fd", hidden, cot_all, preferred_element_type=jnp.float32).astype(
        jnp.bfloat16
    )
    grad_in = lax.psum_scatter(
        jnp.einsum("tf,df->td", pre_grad, w_up, preferred_element_type=jnp.float32),
        ("gx", "gy"),
        scatter_dimension=0,
        tiled=True,
    )
    return (grad_in, grad_up, grad_down)


def solution(mesh):
    placed = (
        P(("gx", "gy"), "gz"),
        P("gz", ("gx", "gy")),
        P(("gx", "gy"), "gz"),
        P(("gx", "gy"), "gz"),
    )
    return jax.shard_map(
        on_device,
        mesh=mesh,
        in_specs=placed,
        out_specs=(P(("gx", "gy"), "gz"), P("gz", ("gx", "gy")), P(("gx", "gy"), "gz")),
        check_vma=False,
    )
```

profile of v0, /device:TPU:8, one launch (start us, length us, event | category | flops | bytes accessed | tf_op | source)
XLA Modules:
  0.0 2198.7 jit_solution(2811474142900817945)
XLA Ops:
  7.2 0.0 copy-start
  7.2 0.0 copy-start.3
  7.2 0.0 all-reduce.7.cloned.1.call-start
  7.2 374.1 %all-gather.1 = bf16[128,3,768]{2,1,0:T(4,128)(2,1)S(1)} all-gather(bf16[1,3,768]{2,1,0:T(4,128)(2,1)} %bitcast.14), channel_id=1, replica_groups=mesh['gx'=16,'gy'=8,'gz'=8] {'gx','gy'}, dimensions={0}, use_global_device_ids=true | all-gather | bytes 594432 | tf_op jit(solution)/shard_map/all_gather | solution.py:24
  381.3 0.5 reshape.9
  381.9 0.0 copy-done.3
  381.9 360.8 %all-gather = bf16[128,3,768]{2,1,0:T(4,128)(2,1)S(1)} all-gather(bf16[1,3,768]{2,1,0:T(4,128)(2,1)S(1)} %bitcast.15), channel_id=1, replica_groups=mesh['gx'=16,'gy'=8,'gz'=8] {'gx','gy'}, dimensions={0}, use_global_device_ids=true | all-gather | bytes 594432 | tf_op jit(solution)/shard_map/all_gather | solution.py:25
  742.7 0.5 reshape.7
  743.2 0.0 copy-done
  743.2 0.0 copy-start.1
  743.2 1.3 fusion.10
  744.5 1.3 fusion.9
  745.8 0.0 all-reduce.7.cloned.1.call-update
  745.8 0.0 all-reduce.5.cloned.1.call-start
  745.9 113.3 %all-reduce.7.cloned.1.call-done = (f32[384,384]{1,0:T(8,128)}, f32[384,384]{1,0:T(8,128)}) async-done(((f32[384,384]{1,0:T(8,128)}, f32[384,384]{1,0:T(8,128)}), (f32[384,384]{1,0:T(8,128)}, f32[384,384]{1,0:T(8,128)})) %all-reduce.7.cloned.1.call-update) | async-done | bytes 1179664 | tf_op jit(solution)/shard_map/psum | solution.py:29
  859.2 1.6 multiply_convert_fusion.1
  860.8 1.5 fusion.11
  862.3 0.0 all-reduce.5.cloned.1.call-update
  862.3 1.3 dynamic-slice
  864.2 0.5 fusion
  864.7 1.1 copy.9
  865.8 1.4 convolution_convert_fusion
  867.2 1323.2 %all-reduce.5.cloned.1.call-done = f32[384,768]{1,0:T(8,128)} async-done(((f32[384,768]{1,0:T(8,128)}), f32[384,768]{1,0:T(8,128)}) %all-reduce.5.cloned.1.call-update) | async-done | bytes 1179664
  2190.4 1.4 constant_dynamic-slice_fusion
  (3 shorter events, 0.0 us)
Async XLA Ops:
  7.2 736.0 %copy-start = (bf16[768,384]{1,0:T(8,128)(2,1)S(1)}, bf16[768,384]{1,0:T(8,128)(2,1)}, u32[]{:S(2)}) copy-start(bf16[768,384]{1,0:T(8,128)(2,1)} %param.5) | copy-start | bytes 1769476
  7.2 374.7 %copy-start.3 = (bf16[3,768]{1,0:T(4,128)(2,1)S(1)}, bf16[3,768]{1,0:T(4,128)(2,1)}, u32[]{:S(2)}) copy-start(bf16[3,768]{1,0:T(4,128)(2,1)} %param.7) | copy-start | bytes 13828
  7.2 852.0 %all-reduce.7.cloned.1.call-start = ((), (), s32[]{:S(2)}) async-start(), calls=%async_computation.1 | async-start | bytes 2359296 | tf_op jit(solution)/shard_map/psum | solution.py:29
  743.2 1.3 copy-start.1
  745.8 1444.6 %all-reduce.5.cloned.1.call-start = ((), (), s32[]{:S(2)}) async-start(), calls=%async_computation | async-start | bytes 2359296
  864.7 1.1 copy-start.2
Sparse Core Ops, SparseCore 0:
  745.9 113.1 all-reduce.6
  862.7 1327.7 all-reduce.4
where the time goes:
time: 2200 us
  waiting for transfers between devices  1440 us (65%)
  blocking collectives  735 us (33%)
    unnamed x3, waiting for transfers between devices  1320 us
    all_gather x1, blocking collectives, on_device(): lax.all_gather(tokens, ('gx', 'gy'), axis=0, tiled=True)  374 us
    all_gather x1, blocking collectives, on_device(): lax.all_gather(cotangent, ('gx', 'gy'), axis=0, tiled=True)  361 us
    psum x1, waiting for transfers between devices, on_device(): pre_act, back_grad = lax.psum((pre_part, back_part), 'gz')  113 us
  transfers between devices with their start and end apart: 2, of which 2 were waited for; matrix products, arithmetic and copies ran while one was open for 0% of the time, Pallas kernels for 0%

commit v1 on v0

v1 whole, which is shorter than its diff:
```python
import functools
import math

import jax
import jax.numpy as jnp
from jax import lax
from jax.experimental import pallas as pl
from jax.experimental.pallas import tpu as pltpu
from jax.sharding import PartitionSpec as P

GELU_SCALE = math.sqrt(2.0 / math.pi)
CUBIC_COEFF = 0.044715
MESH = pl.DeviceIdType.MESH
BF16, F32 = jnp.bfloat16, jnp.float32
CHUNKS = 3


def activate(pre_act, back_grad):
    squared = pre_act * pre_act
    tangent = jnp.tanh(GELU_SCALE * pre_act * (1.0 + CUBIC_COEFF * squared))
    hidden = (0.5 * pre_act * (1.0 + tangent)).astype(BF16)
    gelu_slope = 0.5 * (1.0 + tangent) + 0.5 * pre_act * (1.0 - tangent * tangent) * GELU_SCALE * (
        1.0 + 3.0 * CUBIC_COEFF * squared
    )
    return hidden, (back_grad * gelu_slope).astype(BF16)


def slot_of(offset):
    return 0 if offset == 0 else 2 * offset - 1 if offset > 0 else -2 * offset


def dot_nt(a, b):
    return lax.dot_general(a, b, (((1,), (1,)), ((), ())), preferred_element_type=F32)


def dot_tn(a, b):
    return lax.dot_general(a, b, (((0,), (0,)), ((), ())), preferred_element_type=F32)


def kernel(
    sizes,
    tokens_ref, w_up_ref, w_down_ref, cot_ref,
    grad_in_ref, grad_up_ref, grad_down_ref,
    near, rows, wide, up, down, part, other, z1_out, z1_in, z2_out, z2_in, act,
    back, back_in, own48, last_out, last_in,
    local_sem, near_send, near_recv, y_send, y_recv, core_send, core_recv,
    z_send, z_recv, act_send, act_recv, back_send, back_recv, last_send, last_recv,
):
    n_gx, n_gy, n_gz = sizes
    n_hi = n_gz // 2
    own_rows = tokens_ref.shape[0]
    slot_rows = n_gx * own_rows
    total_rows = n_gy * slot_rows
    chunk_rows = total_rows // CHUNKS
    gx, gy, gz = lax.axis_index("gx"), lax.axis_index("gy"), lax.axis_index("gz")
    hi, core = gz // 2, gz % 2

    def at_gx(j):
        return ((gx + j) % n_gx, gy, gz)

    def at_gy(j):
        return (gx, (gy + n_gy + j) % n_gy, gz)

    def at_hi(j):
        return (gx, gy, ((hi + n_hi + j) % n_hi) * 2 + core)

    other_core = (gx, gy, hi * 2 + 1 - core)

    load_up = pltpu.make_async_copy(w_up_ref, up, local_sem.at[0])
    load_down = pltpu.make_async_copy(w_down_ref, down, local_sem.at[1])
    load_tokens = pltpu.make_async_copy(tokens_ref, near.at[gx, 0], local_sem.at[2])
    load_cot = pltpu.make_async_copy(cot_ref, near.at[gx, 1], local_sem.at[3])
    load_tokens.start()
    load_cot.start()
    load_up.start()
    load_down.start()

    partners = [at_gx(j) for j in range(1, n_gx)] + [at_gy(j) for j in range(1, n_gy)]
    partners += [at_hi(1), at_hi(-1), other_core]
    barrier = pltpu.get_barrier_semaphore()
    for partner in partners:
        pl.semaphore_signal(barrier, inc=1, device_id=partner, device_id_type=MESH)
    load_tokens.wait()
    load_cot.wait()
    pl.semaphore_wait(barrier, len(partners))

    sent = []

    def send(src, dst, send_sem, recv_sem, device):
        copy = pltpu.make_async_remote_copy(
            src_ref=src, dst_ref=dst, send_sem=send_sem, recv_sem=recv_sem, device_id=device, device_id_type=MESH
        )
        copy.start()
        sent.append(copy)

    def arrived(dst, recv_sem):
        pltpu.make_async_remote_copy(
            src_ref=dst, dst_ref=dst, send_sem=recv_sem, recv_sem=recv_sem, device_id=other_core, device_id_type=MESH
        ).wait_recv()

    for j in range(1, n_gx):
        send(near.at[gx], near.at[gx], near_send.at[j], near_recv.at[j], at_gx(j))
    for j in range(1, n_gx):
        arrived(near.at[(gx + n_gx - j) % n_gx], near_recv.at[j])
    for u in range(n_gx):
        for which in range(2):
            wide[which, u * own_rows : (u + 1) * own_rows] = near[u, which].astype(F32)
    rows[:, :slot_rows] = wide[...].astype(BF16)

    half = n_gy // 2
    split = slot_rows // 3 // 16 * 16

    def slot(offset, start=0, stop=slot_rows):
        first = slot_of(offset) * slot_rows
        return rows.at[:, first + start : first + stop]

    def ring(step):
        if step < half:
            send(slot(step - 1), slot(step), y_send.at[0, step], y_recv.at[0, step], at_gy(-1))
            send(slot(1 - step), slot(-step), y_send.at[1, step], y_recv.at[1, step], at_gy(1))
        else:
            lower, upper = (0, split), (split, slot_rows)
            send(slot(half - 1, *upper), slot(half, *upper), y_send.at[0, step], y_recv.at[0, step], at_gy(-1))
            send(slot(1 - half, *lower), slot(half, *lower), y_send.at[1, step], y_recv.at[1, step], at_gy(1))

    def ring_arrived(step):
        if step < half:
            arrived(slot(step), y_recv.at[0, step])
            arrived(slot(-step), y_recv.at[1, step])
        else:
            arrived(slot(half, split, slot_rows), y_recv.at[0, step])
            arrived(slot(half, 0, split), y_recv.at[1, step])

    right, left, across = (hi + 1) % n_hi, (hi + n_hi - 1) % n_hi, (hi + 2) % n_hi

    def chunk(c):
        return pl.ds(c * chunk_rows, chunk_rows)

    def forward(c):
        for which, value in enumerate(
            (
                jnp.dot(rows[0, chunk(c)], up[...], preferred_element_type=F32),
                dot_nt(rows[1, chunk(c)], down[...]),
            )
        ):
            part[c, :, which] = value.reshape(n_gz, chunk_rows // n_gz, value.shape[1])
        theirs = part.at[c, pl.ds((1 - core) * n_hi, n_hi)]
        send(theirs, other.at[c], core_send.at[c, 0], core_recv.at[c, 0], other_core)

    def mine(c, h, which):
        return part[c, core * n_hi + h, which] + other[c, h, which]

    def z1(c):
        arrived(other.at[c], core_recv.at[c, 0])
        for which, to in ((0, 1), (1, -1)):
            z1_out[c, which] = mine(c, across, which).astype(BF16)
            send(z1_out.at[c, which], z1_in.at[c, which], z_send.at[c, which], z_recv.at[c, which], at_hi(to))

    def z2(c):
        arrived(z1_in.at[c, 0], z_recv.at[c, 0])
        z2_out[c, 0, 0] = (mine(c, right, 0) + z1_in[c, 0].astype(F32)).astype(BF16)
        z2_out[c, 0, 1] = mine(c, right, 1).astype(BF16)
        send(z2_out.at[c, 0], z2_in.at[c, 0], z_send.at[c, 2], z_recv.at[c, 2], at_hi(1))
        arrived(z1_in.at[c, 1], z_recv.at[c, 1])
        z2_out[c, 1, 0] = mine(c, left, 0).astype(BF16)
        z2_out[c, 1, 1] = (mine(c, left, 1) + z1_in[c, 1].astype(F32)).astype(BF16)
        send(z2_out.at[c, 1], z2_in.at[c, 1], z_send.at[c, 3], z_recv.at[c, 3], at_hi(-1))

    def held(c, h, k=core):
        return act.at[c, k * n_hi + h]

    def to_core(c, h, at):
        send(held(c, h), held(c, h), core_send.at[c, at], core_recv.at[c, at], other_core)

    def z3(c):
        arrived(z2_in.at[c, 0], z_recv.at[c, 2])
        arrived(z2_in.at[c, 1], z_recv.at[c, 3])
        pre_act, back_grad = (
            mine(c, hi, which) + z2_in[c, 0, which].astype(F32) + z2_in[c, 1, which].astype(F32) for which in range(2)
        )
        hidden, pre_grad = activate(pre_act, back_grad)
        act[c, gz % 2 * n_hi + hi, 0] = hidden
        act[c, gz % 2 * n_hi + hi, 1] = pre_grad
        send(held(c, hi), held(c, hi), act_send.at[c, 0], act_recv.at[c, 0], at_hi(1))
        send(held(c, hi), held(c, hi), act_send.at[c, 1], act_recv.at[c, 1], at_hi(-1))
        to_core(c, hi, 1)

    def z4(c):
        arrived(held(c, left), act_recv.at[c, 0])
        send(held(c, left).at[0], held(c, left).at[0], act_send.at[c, 2], act_recv.at[c, 2], at_hi(1))
        arrived(held(c, right), act_recv.at[c, 1])
        send(held(c, right).at[1], held(c, right).at[1], act_send.at[c, 3], act_recv.at[c, 3], at_hi(-1))
        to_core(c, left, 2)
        to_core(c, right, 3)

    def z5(c):
        arrived(held(c, across).at[0], act_recv.at[c, 2])
        arrived(held(c, across).at[1], act_recv.at[c, 3])
        to_core(c, across, 4)
        for at, h in ((1, hi), (2, left), (3, right), (4, across)):
            arrived(held(c, h, 1 - core), core_recv.at[c, at])

    def whole(c, which):
        return act[c, :, which].reshape(chunk_rows, act.shape[-1])

    tile = 16
    done = []

    def backward(c):
        value = dot_nt(whole(c, 1), up[...])
        first = c * chunk_rows
        back[first : first + chunk_rows] = value.astype(BF16)
        if c == 0:
            own48[...] = value[:slot_rows]
        for offset in range(1 - half, half + 1):
            at = slot_of(offset)
            if at and at not in done and (at + 1) * slot_rows <= first + chunk_rows:
                done.append(at)
                send(
                    back.at[at * slot_rows : (at + 1) * slot_rows], back_in.at[at],
                    back_send.at[at], back_recv.at[at], at_gy(offset),
                )

    ring(1)
    load_up.wait()
    load_down.wait()
    ring_arrived(1)
    ring(2)
    forward(0)
    ring_arrived(2)
    ring(3)
    z1(0)
    ring_arrived(3)
    ring(4)
    forward(1)
    z2(0)
    z1(1)
    ring_arrived(4)
    forward(2)
    z3(0)
    z2(1)
    z1(2)
    z4(0)
    z3(1)
    z2(2)
    z5(0)
    backward(0)
    z4(1)
    z3(2)
    z5(1)
    backward(1)
    z4(2)
    z5(2)
    backward(2)

    hidden = jnp.concatenate([whole(c, 0) for c in range(CHUNKS)])
    pre_grad = jnp.concatenate([whole(c, 1) for c in range(CHUNKS)])
    grad_up_ref[...] = dot_tn(rows[0], pre_grad).astype(BF16)
    grad_down_ref[...] = dot_tn(hidden, rows[1]).astype(BF16)

    for at in range(1, n_gy):
        arrived(back_in.at[at], back_recv.at[at])
        own48[...] += back_in[at].astype(F32)
    for u in range(n_gx):
        last_out[u] = own48[u * own_rows : (u + 1) * own_rows].astype(BF16)
    for j in range(1, n_gx):
        send(last_out.at[(gx + j) % n_gx], last_in.at[j], last_send.at[j], last_recv.at[j], at_gx(j))
    result = last_out[gx].astype(F32)
    for j in range(1, n_gx):
        arrived(last_in.at[j], last_recv.at[j])
        result += last_in[j].astype(F32)
    grad_in_ref[...] = result
    for copy in sent:
        copy.wait_send()


def on_device(sizes, tokens, w_up, w_down, cotangent):
    n_gx, n_gy, n_gz = sizes
    own_rows, width = tokens.shape
    units = w_up.shape[1]
    slot_rows = n_gx * own_rows
    total = slot_rows * n_gy
    n_hi = n_gz // 2
    r = total // CHUNKS // n_gz
    dma = pltpu.SemaphoreType.DMA
    return pl.pallas_call(
        functools.partial(kernel, sizes),
        out_shape=(
            jax.ShapeDtypeStruct((own_rows, width), F32),
            jax.ShapeDtypeStruct((width, units), BF16),
            jax.ShapeDtypeStruct((units, width), BF16),
        ),
        in_specs=[pl.BlockSpec(memory_space=pl.ANY)] * 4,
        out_specs=(pl.BlockSpec(memory_space=pltpu.VMEM),) * 3,
        scratch_shapes=[
            pltpu.VMEM((n_gx, 2, own_rows, width), BF16),
            pltpu.VMEM((2, total, width), BF16),
            pltpu.VMEM((2, slot_rows, width), F32),
            pltpu.VMEM((width, units), BF16),
            pltpu.VMEM((units, width), BF16),
            pltpu.VMEM((CHUNKS, n_gz, 2, r, units), F32),
            pltpu.VMEM((CHUNKS, n_hi, 2, r, units), F32),
            pltpu.VMEM((CHUNKS, 2, r, units), BF16),
            pltpu.VMEM((CHUNKS, 2, r, units), BF16),
            pltpu.VMEM((CHUNKS, 2, 2, r, units), BF16),
            pltpu.VMEM((CHUNKS, 2, 2, r, units), BF16),
            pltpu.VMEM((CHUNKS, n_gz, 2, r, units), BF16),
            pltpu.VMEM((total, width), BF16),
            pltpu.VMEM((n_gy, slot_rows, width), BF16),
            pltpu.VMEM((slot_rows, width), F32),
            pltpu.VMEM((n_gx, own_rows, width), BF16),
            pltpu.VMEM((n_gx, own_rows, width), BF16),
            dma((4,)),
            dma((n_gx,)),
            dma((n_gx,)),
            dma((2, n_gy // 2 + 1)),
            dma((2, n_gy // 2 + 1)),
            dma((CHUNKS, 5)),
            dma((CHUNKS, 5)),
            dma((CHUNKS, 4)),
            dma((CHUNKS, 4)),
            dma((CHUNKS, 4)),
            dma((CHUNKS, 4)),
            dma((n_gy,)),
            dma((n_gy,)),
            dma((n_gx,)),
            dma((n_gx,)),
        ],
        compiler_params=pltpu.CompilerParams(
            collective_id=0, has_side_effects=True, vmem_limit_bytes=48 * 1024 * 1024
        ),
    )(tokens, w_up, w_down, cotangent)


def solution(mesh):
    sizes = tuple(mesh.shape[axis] for axis in ("gx", "gy", "gz"))
    placed = (
        P(("gx", "gy"), "gz"),
        P("gz", ("gx", "gy")),
        P(("gx", "gy"), "gz"),
        P(("gx", "gy"), "gz"),
    )
    return jax.shard_map(
        functools.partial(on_device, sizes),
        mesh=mesh,
        in_specs=placed,
        out_specs=(P(("gx", "gy"), "gz"), P("gz", ("gx", "gy")), P(("gx", "gy"), "gz")),
        check_vma=False,
    )
```

time: 2200 us -> 103 us (0.05)
  the two profiles are of different devices: /device:TPU:8 before, /device:TPU:1 now
where the time goes in v1:
time: 103 us
  Pallas kernels  96.4 us (94%)
  local copies, waits for them, and re-layouts  5.73 us (6%)
    pallas_call x1, Pallas kernels, on_device(): pl.pallas_call(functools.partial(kernel, sizes), out_shape=(jax.ShapeDtyp...  96.4 us
    unnamed x11, local copies, waits for them, and re-layouts  5.73 us

profile of v1, /device:TPU:1, one launch (start us, length us, event | category | flops | bytes accessed | tf_op | source)
XLA Modules:
  0.0 102.8 jit_solution(11799370140200335005)
XLA Ops:
  0.6 0.0 copy-start
  0.6 1.1 %copy-done = bf16[768,384]{1,0:T(8,128)(2,1)S(1)} copy-done((bf16[768,384]{1,0:T(8,128)(2,1)S(1)}, bf16[768,384]{1,0:T(8,128)(2,1)}, u32[]{:S(2)}) %copy-start) | copy-done | bytes 589848
  1.7 0.0 copy-start.1
  1.7 1.1 %copy-done.1 = bf16[384,768]{1,0:T(8,128)(2,1)S(1)} copy-done((bf16[384,768]{1,0:T(8,128)(2,1)S(1)}, bf16[384,768]{1,0:T(8,128)(2,1)}, u32[]{:S(2)}) %copy-start.1) | copy-done | bytes 589848
  2.8 0.0 copy-start.2
  2.8 0.7 copy-done.2
  3.5 0.0 copy-start.3
  3.5 0.7 copy-done.3
  4.1 96.4 %shard_map.67 = (f32[3,768]{1,0:T(4,128)S(1)}, bf16[768,384]{1,0:T(8,128)(2,1)S(1)}, bf16[384,768]{1,0:T(8,128)(2,1)S(1)}) custom-call(bf16[3,768]{1,0:T(4,128)(2,1)S(1)} %copy-done.2, bf16[768,384]{1,0:T(8,128)(2,1)S(1)} %copy-done, bf16[384,768]{1,0:T(8,128)(2,1)S(1)} %copy-done.1, bf16[3,768]{1,0:T(4,128)(2,1)S(1)} %copy-done.3), custom_call_target="tpu_custom_call" | custom-call | tf_op jit(solution)/shard_map/pallas_call | solution.py:286
  100.5 0.6 copy.10
  101.1 0.8 copy.11
  102.0 0.8 copy.12
Async XLA Ops:
  0.6 1.1 %copy-start = (bf16[768,384]{1,0:T(8,128)(2,1)S(1)}, bf16[768,384]{1,0:T(8,128)(2,1)}, u32[]{:S(2)}) copy-start(bf16[768,384]{1,0:T(8,128)(2,1)} %w_up_ref.1) | copy-start | bytes 1769476
  1.7 1.1 %copy-start.1 = (bf16[384,768]{1,0:T(8,128)(2,1)S(1)}, bf16[384,768]{1,0:T(8,128)(2,1)}, u32[]{:S(2)}) copy-start(bf16[384,768]{1,0:T(8,128)(2,1)} %w_down_ref.1) | copy-start | bytes 1769476
  2.8 0.7 copy-start.2
  3.5 0.7 copy-start.3

commit v2 on v1

--- a/solution.py
+++ b/solution.py
@@ -110,26 +110,30 @@
     half = n_gy // 2
     split = slot_rows // 3 // 16 * 16
 
-    def slot(offset, start=0, stop=slot_rows):
+    def slot(which, offset, start=0, stop=slot_rows):
         first = slot_of(offset) * slot_rows
-        return rows.at[:, first + start : first + stop]
-
-    def ring(step):
+        return rows.at[which, first + start : first + stop]
+
+    def hops(which, step):
         if step < half:
-            send(slot(step - 1), slot(step), y_send.at[0, step], y_recv.at[0, step], at_gy(-1))
-            send(slot(1 - step), slot(-step), y_send.at[1, step], y_recv.at[1, step], at_gy(1))
+            lower = upper = (0, slot_rows)
         else:
             lower, upper = (0, split), (split, slot_rows)
-            send(slot(half - 1, *upper), slot(half, *upper), y_send.at[0, step], y_recv.at[0, step], at_gy(-1))
-            send(slot(1 - half, *lower), slot(half, *lower), y_send.at[1, step], y_recv.at[1, step], at_gy(1))
-
-    def ring_arrived(step):
-        if step < half:
-            arrived(slot(step), y_recv.at[0, step])
-            arrived(slot(-step), y_recv.at[1, step])
-        else:
-            arrived(slot(half, split, slot_rows), y_recv.at[0, step])
-            arrived(slot(half, 0, split), y_recv.at[1, step])
+        return (
+            (slot(which, step - 1, *upper), slot(which, step, *upper), -1),
+            (slot(which, 1 - step, *lower), slot(which, -step if step < half else half, *lower), 1),
+        )
+
+    def ring(which, step):
+        for way, (src, dst, to) in enumerate(hops(which, step)):
+            send(src, dst, y_send.at[way, which, step], y_recv.at[way, which, step], at_gy(to))
+
+    def pass_on(step):
+        for which in range(2):
+            for way, (_, dst, _) in enumerate(hops(which, step)):
+                arrived(dst, y_recv.at[way, which, step])
+            if step < half:
+                ring(which, step + 1)
 
     right, left, across = (hi + 1) % n_hi, (hi + n_hi - 1) % n_hi, (hi + 2) % n_hi
 
@@ -197,6 +201,8 @@
         arrived(held(c, across).at[0], act_recv.at[c, 2])
         arrived(held(c, across).at[1], act_recv.at[c, 3])
         to_core(c, across, 4)
+
+    def z6(c):
         for at, h in ((1, hi), (2, left), (3, right), (4, across)):
             arrived(held(c, h, 1 - core), core_recv.at[c, at])
 
@@ -221,36 +227,37 @@
                     back_send.at[at], back_recv.at[at], at_gy(offset),
                 )
 
-    ring(1)
+    ring(0, 1)
+    ring(1, 1)
     load_up.wait()
     load_down.wait()
-    ring_arrived(1)
-    ring(2)
+    pass_on(1)
     forward(0)
-    ring_arrived(2)
-    ring(3)
+    pass_on(2)
     z1(0)
-    ring_arrived(3)
-    ring(4)
+    pass_on(3)
     forward(1)
     z2(0)
+    pass_on(4)
     z1(1)
-    ring_arrived(4)
     forward(2)
+    z1(2)
     z3(0)
     z2(1)
-    z1(2)
+    z2(2)
     z4(0)
     z3(1)
-    z2(2)
+    z3(2)
     z5(0)
+    z4(1)
+    z6(0)
     backward(0)
-    z4(1)
-    z3(2)
+    z4(2)
     z5(1)
+    z6(1)
     backward(1)
-    z4(2)
     z5(2)
+    z6(2)
     backward(2)
 
     hidden = jnp.concatenate([whole(c, 0) for c in range(CHUNKS)])
@@ -290,7 +297,7 @@
             jax.ShapeDtypeStruct((width, units), BF16),
             jax.ShapeDtypeStruct((units, width), BF16),
         ),
-        in_specs=[pl.BlockSpec(memory_space=pl.ANY)] * 4,
+        in_specs=[pl.BlockSpec(memory_space=pltpu.HBM)] * 4,
         out_specs=(pl.BlockSpec(memory_space=pltpu.VMEM),) * 3,
         scratch_shapes=[
             pltpu.VMEM((n_gx, 2, own_rows, width), BF16),
@@ -313,8 +320,8 @@
             dma((4,)),
             dma((n_gx,)),
             dma((n_gx,)),
-            dma((2, n_gy // 2 + 1)),
-            dma((2, n_gy // 2 + 1)),
+            dma((2, 2, n_gy // 2 + 1)),
+            dma((2, 2, n_gy // 2 + 1)),
             dma((CHUNKS, 5)),
             dma((CHUNKS, 5)),
             dma((CHUNKS, 4)),

time: 103 us -> 100 us (0.971)
  Pallas kernels: 96.4 us -> 93.1 us
    pallas_call x1, Pallas kernels: 96.4 us -> 93.1 us  [on_device(): pl.pallas_call(functools.partial(kernel, sizes), out_shape=(jax.ShapeDtyp...]
where the time goes in v2:
time: 100 us; the launch traced here: 99.5 us
  Pallas kernels  93.1 us (93%)
  local copies, waits for them, and re-layouts  5.73 us (6%)
    pallas_call x1, Pallas kernels, on_device(): pl.pallas_call(functools.partial(kernel, sizes), out_shape=(jax.ShapeDtyp...  93.1 us
    unnamed x11, local copies, waits for them, and re-layouts  5.73 us

profile of v2, /device:TPU:1, one launch (start us, length us, event | category | flops | bytes accessed | tf_op | source)
XLA Modules:
  0.0 99.5 jit_solution(13697289814327189877)
XLA Ops:
  0.6 0.0 copy-start
  0.6 1.1 %copy-done = bf16[768,384]{1,0:T(8,128)(2,1)S(1)} copy-done((bf16[768,384]{1,0:T(8,128)(2,1)S(1)}, bf16[768,384]{1,0:T(8,128)(2,1)}, u32[]{:S(2)}) %copy-start) | copy-done | bytes 589848
  1.7 0.0 copy-start.1
  1.7 1.1 %copy-done.1 = bf16[384,768]{1,0:T(8,128)(2,1)S(1)} copy-done((bf16[384,768]{1,0:T(8,128)(2,1)S(1)}, bf16[384,768]{1,0:T(8,128)(2,1)}, u32[]{:S(2)}) %copy-start.1) | copy-done | bytes 589848
  2.8 0.0 copy-start.2
  2.8 0.7 copy-done.2
  3.5 0.0 copy-start.3
  3.5 0.7 copy-done.3
  4.1 93.1 %shard_map.67 = (f32[3,768]{1,0:T(4,128)S(1)}, bf16[768,384]{1,0:T(8,128)(2,1)S(1)}, bf16[384,768]{1,0:T(8,128)(2,1)S(1)}) custom-call(bf16[3,768]{1,0:T(4,128)(2,1)S(1)} %copy-done.2, bf16[768,384]{1,0:T(8,128)(2,1)S(1)} %copy-done, bf16[384,768]{1,0:T(8,128)(2,1)S(1)} %copy-done.1, bf16[3,768]{1,0:T(4,128)(2,1)S(1)} %copy-done.3), custom_call_target="tpu_custom_call" | custom-call | tf_op jit(solution)/shard_map/pallas_call | solution.py:293
  97.3 0.6 copy.10
  97.9 0.8 copy.11
  98.7 0.8 copy.12
Async XLA Ops:
  0.6 1.1 %copy-start = (bf16[768,384]{1,0:T(8,128)(2,1)S(1)}, bf16[768,384]{1,0:T(8,128)(2,1)}, u32[]{:S(2)}) copy-start(bf16[768,384]{1,0:T(8,128)(2,1)} %w_up_ref.1) | copy-start | bytes 1769476
  1.7 1.1 %copy-start.1 = (bf16[384,768]{1,0:T(8,128)(2,1)S(1)}, bf16[384,768]{1,0:T(8,128)(2,1)}, u32[]{:S(2)}) copy-start(bf16[384,768]{1,0:T(8,128)(2,1)} %w_down_ref.1) | copy-start | bytes 1769476
  2.8 0.7 copy-start.2
  3.5 0.7 copy-start.3

commit v3 on v2

v3 whole, which is shorter than its diff:
```python
import functools
import math

import jax
import jax.numpy as jnp
from jax import lax
from jax.experimental import pallas as pl
from jax.experimental.pallas import tpu as pltpu
from jax.sharding import PartitionSpec as P

GELU_SCALE = math.sqrt(2.0 / math.pi)
CUBIC_COEFF = 0.044715
MESH = pl.DeviceIdType.MESH
BF16, F32 = jnp.bfloat16, jnp.float32
CHUNKS = 3
PIECES = 3
VMEM_LIMIT = 63 * 1024 * 1024
N_X = 4


def activate(pre_act, back_grad):
    squared = pre_act * pre_act
    tangent = jnp.tanh(GELU_SCALE * pre_act * (1.0 + CUBIC_COEFF * squared))
    hidden = (0.5 * pre_act * (1.0 + tangent)).astype(BF16)
    gelu_slope = 0.5 * (1.0 + tangent) + 0.5 * pre_act * (1.0 - tangent * tangent) * GELU_SCALE * (
        1.0 + 3.0 * CUBIC_COEFF * squared
    )
    return hidden, (back_grad * gelu_slope).astype(BF16)


def slot_of(offset):
    return 0 if offset == 0 else 2 * offset - 1 if offset > 0 else -2 * offset


def dot_nt(a, b):
    return lax.dot_general(a, b, (((1,), (1,)), ((), ())), preferred_element_type=F32)


def dot_tn(a, b):
    return lax.dot_general(a, b, (((0,), (0,)), ((), ())), preferred_element_type=F32)


def kernel(
    sizes,
    tokens_ref, w_up_ref, w_down_ref, cot_ref,
    grad_in_ref, grad_up_ref, grad_down_ref,
    near, rows, wide, up, down, part, other, act,
    pair_sum, pair_out, pair_in, back, x_out, x_in, back_out, back_in, own_sum, last_out, last_in, grad_up, grad_down,
    local_sem, near_send, near_recv, y_send, y_recv, core_send, core_recv,
    z_send, z_recv, x_send, x_recv, back_send, back_recv, last_send, last_recv,
):
    n_gx, n_gy, n_gz = sizes
    n_hi = n_gz // 2
    own_rows = tokens_ref.shape[0]
    slot_rows = n_gx * own_rows
    total_rows = n_gy * slot_rows
    chunk_rows = total_rows // CHUNKS
    gx, gy, gz = lax.axis_index("gx"), lax.axis_index("gy"), lax.axis_index("gz")
    hi, core = gz // 2, gz % 2
    n_low = n_gx // N_X
    at_x, low = gx // n_low, gx % n_low

    def at_gx(j):
        return ((at_x + j // n_low) % N_X * n_low + (low + j % n_low) % n_low, gy, gz)

    def at_gy(j):
        return (gx, (gy + n_gy + j) % n_gy, gz)

    def at_hi(j):
        return (gx, gy, ((hi + n_hi + j) % n_hi) * 2 + core)

    other_core = (gx, gy, hi * 2 + 1 - core)

    load_up = pltpu.make_async_copy(w_up_ref, up, local_sem.at[0])
    load_down = pltpu.make_async_copy(w_down_ref, down, local_sem.at[1])
    load_tokens = pltpu.make_async_copy(tokens_ref, near.at[0, 0], local_sem.at[2])
    load_cot = pltpu.make_async_copy(cot_ref, near.at[0, 1], local_sem.at[3])
    load_tokens.start()
    load_cot.start()
    load_up.start()
    load_down.start()

    partners = [at_gx(j) for j in range(1, n_gx)] + [at_gy(j) for j in range(1, n_gy)]
    partners += [at_hi(1), at_hi(-1), other_core]
    barrier = pltpu.get_barrier_semaphore()
    for partner in partners:
        pl.semaphore_signal(barrier, inc=1, device_id=partner, device_id_type=MESH)
    load_tokens.wait()
    load_cot.wait()
    pl.semaphore_wait(barrier, len(partners))

    sent = []

    def send(src, dst, send_sem, recv_sem, device):
        copy = pltpu.make_async_remote_copy(
            src_ref=src, dst_ref=dst, send_sem=send_sem, recv_sem=recv_sem, device_id=device, device_id_type=MESH
        )
        copy.start()
        sent.append(copy)

    def arrived(dst, recv_sem):
        pltpu.make_async_remote_copy(
            src_ref=dst, dst_ref=dst, send_sem=recv_sem, recv_sem=recv_sem, device_id=other_core, device_id_type=MESH
        ).wait_recv()

    for j in range(1, n_gx):
        send(near.at[0], near.at[j], near_send.at[j], near_recv.at[j], at_gx(j))
    for j in range(n_gx):
        if j:
            arrived(near.at[j], near_recv.at[j])
        for which in range(2):
            wide[which, j * own_rows : (j + 1) * own_rows] = near[j, which].astype(F32)
    rows[:, :slot_rows] = wide[...].astype(BF16)

    half = n_gy // 2
    piece = slot_rows // PIECES

    def hop(step, which, at, way):
        offset = step if way == 0 or step == half else -step
        before = step - 1 if way == 0 else 1 - step
        src, dst = (slot_of(o) * slot_rows + at * piece for o in (before, offset))
        return rows.at[which, src : src + piece], rows.at[which, dst : dst + piece]

    def travels(step, which, way):
        return step < half or which == way

    def ring(step, which, at, way):
        src, dst = hop(step, which, at, way)
        sems = (way, which, at, step)
        send(src, dst, y_send.at[sems], y_recv.at[sems], at_gy(-1 if way == 0 else 1))

    order = [(which, at, way) for at in range(PIECES) for which in range(2) for way in range(2)]

    def pass_on(step):
        for which, at, way in order:
            if step and travels(step, which, way):
                arrived(hop(step, which, at, way)[1], y_recv.at[way, which, at, step])
            if step < half and travels(step + 1, which, way):
                ring(step + 1, which, at, way)

    def chunk(c):
        return pl.ds(c * chunk_rows, chunk_rows)

    def forward(c):
        for which, value in enumerate(
            (
                jnp.dot(rows[0, chunk(c)], up[...], preferred_element_type=F32),
                dot_nt(rows[1, chunk(c)], down[...]),
            )
        ):
            part[c, :, which] = value.reshape(n_gz, chunk_rows // n_gz, value.shape[1])
        theirs = part.at[c, pl.ds((1 - core) * n_hi, n_hi)]
        send(theirs, other.at[c], core_send.at[c, 0], core_recv.at[c, 0], other_core)

    towards = 1 - 2 * (hi % 2)

    def pair_send(c, step, which):
        pair_out[c, step, which] = pair_sum[c, which].astype(BF16)
        to = towards if (step + which) % 2 == 0 else -towards
        send(
            pair_out.at[c, step, which], pair_in.at[c, step, which],
            z_send.at[c, 2 * step + which], z_recv.at[c, 2 * step + which], at_hi(to),
        )

    def pair_add(c, step, which):
        arrived(pair_in.at[c, step, which], z_recv.at[c, 2 * step + which])
        pair_sum[c, which] += pair_in[c, step, which].astype(F32)

    def e1(c):
        arrived(other.at[c], core_recv.at[c, 0])
        for which in range(2):
            pair_sum[c, which] = part[c, pl.ds(core * n_hi, n_hi), which] + other[c, :, which]
            pair_send(c, 0, which)

    def e2(c):
        for which in range(2):
            pair_add(c, 0, which)
            pair_send(c, 1, which)

    def e3(c):
        for which in range(2):
            pair_add(c, 1, which)
        hidden, pre_grad = activate(pair_sum[c, 0], pair_sum[c, 1])
        act[c, pl.ds(core * n_hi, n_hi), 0] = hidden
        act[c, pl.ds(core * n_hi, n_hi), 1] = pre_grad
        mine_all = act.at[c, pl.ds(core * n_hi, n_hi)]
        send(mine_all, mine_all, core_send.at[c, 1], core_recv.at[c, 1], other_core)

    def e6(c):
        arrived(act.at[c, pl.ds((1 - core) * n_hi, n_hi)], core_recv.at[c, 1])

    def whole(c, which):
        return act[c, :, which].reshape(chunk_rows, act.shape[-1])

    x_rows = slot_rows // N_X
    slots = {slot_of(offset): offset for offset in range(1 - half, half + 1)}

    def finished(c):
        return [at for at in slots if c * chunk_rows < (at + 1) * slot_rows <= (c + 1) * chunk_rows]

    def group(at, j):
        start = at * slot_rows + j * x_rows
        return back[start : start + x_rows]

    def backward(c):
        first = c * chunk_rows
        back[first : first + chunk_rows] = dot_nt(whole(c, 1), up[...])
        done = sorted(finished(c))
        for j in range(1, N_X):
            for i, at in enumerate(done):
                x_out[c, j, i] = group(at, j).astype(BF16)
            send(
                x_out.at[c, j, pl.ds(0, len(done))], x_in.at[c, j, pl.ds(0, len(done))],
                x_send.at[c, j], x_recv.at[c, j], at_gx((N_X - j) * n_low),
            )

    def sum_x(c):
        done = sorted(finished(c))
        for j in range(1, N_X):
            arrived(x_in.at[c, j, pl.ds(0, len(done))], x_recv.at[c, j])
        for i, at in enumerate(done):
            total = group(at, 0)
            for j in range(1, N_X):
                total += x_in[c, j, i].astype(F32)
            if at == 0:
                own_sum[...] = total
            else:
                back_out[at] = total.astype(BF16)
                send(back_out.at[at], back_in.at[at], back_send.at[at], back_recv.at[at], at_gy(slots[at]))

    pass_on(0)
    load_up.wait()
    load_down.wait()
    pass_on(1)
    forward(0)
    pass_on(2)
    e1(0)
    pass_on(3)
    forward(1)
    pass_on(4)
    e1(1)
    forward(2)
    e2(0)
    e1(2)
    e2(1)
    e3(0)
    e2(2)
    e6(0)
    backward(0)
    e3(1)
    e6(1)
    backward(1)
    e3(2)
    sum_x(0)
    e6(2)
    backward(2)
    sum_x(1)
    sum_x(2)

    hidden = jnp.concatenate([whole(c, 0) for c in range(CHUNKS)])
    pre_grad = jnp.concatenate([whole(c, 1) for c in range(CHUNKS)])
    grad_up[...] = dot_tn(rows[0], pre_grad).astype(BF16)
    store_up = pltpu.make_async_copy(grad_up, grad_up_ref, local_sem.at[0])
    store_up.start()
    grad_down[...] = dot_tn(hidden, rows[1]).astype(BF16)
    store_down = pltpu.make_async_copy(grad_down, grad_down_ref, local_sem.at[1])
    store_down.start()

    for at in range(1, n_gy):
        arrived(back_in.at[at], back_recv.at[at])
        own_sum[...] += back_in[at].astype(F32)
    for j in range(1, n_low):
        last_out[j] = own_sum[j * own_rows : (j + 1) * own_rows].astype(BF16)
        send(last_out.at[j], last_in.at[j], last_send.at[j], last_recv.at[j], at_gx(n_low - j))
    result = own_sum[:own_rows]
    for j in range(1, n_low):
        arrived(last_in.at[j], last_recv.at[j])
        result += last_in[j].astype(F32)
    grad_in_ref[...] = result
    store_up.wait()
    store_down.wait()
    for copy in sent:
        copy.wait_send()


def hand_over(*refs):
    for src, dst in zip(refs[:3], refs[3:]):
        dst[...] = src[...]


def on_device(sizes, tokens, w_up, w_down, cotangent):
    n_gx, n_gy, n_gz = sizes
    own_rows, width = tokens.shape
    units = w_up.shape[1]
    slot_rows = n_gx * own_rows
    total = slot_rows * n_gy
    n_hi = n_gz // 2
    r = total // CHUNKS // n_gz
    n_low, x_rows = n_gx // N_X, slot_rows // N_X
    dma = pltpu.SemaphoreType.DMA
    results = pl.pallas_call(
        functools.partial(kernel, sizes),
        out_shape=(
            jax.ShapeDtypeStruct((own_rows, width), F32),
            jax.ShapeDtypeStruct((width, units), BF16),
            jax.ShapeDtypeStruct((units, width), BF16),
        ),
        in_specs=[pl.BlockSpec(memory_space=pltpu.HBM)] * 4,
        out_specs=(
            pl.BlockSpec(memory_space=pltpu.VMEM),
            pl.BlockSpec(memory_space=pl.ANY),
            pl.BlockSpec(memory_space=pl.ANY),
        ),
        scratch_shapes=[
            pltpu.VMEM((n_gx, 2, own_rows, width), BF16),
            pltpu.VMEM((2, total, width), BF16),
            pltpu.VMEM((2, slot_rows, width), F32),
            pltpu.VMEM((width, units), BF16),
            pltpu.VMEM((units, width), BF16),
            pltpu.VMEM((CHUNKS, n_gz, 2, r, units), F32),
            pltpu.VMEM((CHUNKS, n_hi, 2, r, units), F32),
            pltpu.VMEM((CHUNKS, n_gz, 2, r, units), BF16),
            pltpu.VMEM((CHUNKS, 2, n_hi, r, units), F32),
            pltpu.VMEM((CHUNKS, 2, 2, n_hi, r, units), BF16),
            pltpu.VMEM((CHUNKS, 2, 2, n_hi, r, units), BF16),
            pltpu.VMEM((total, width), F32),
            pltpu.VMEM((CHUNKS, N_X, n_gy // 2, x_rows, width), BF16),
            pltpu.VMEM((CHUNKS, N_X, n_gy // 2, x_rows, width), BF16),
            pltpu.VMEM((n_gy, x_rows, width), BF16),
            pltpu.VMEM((n_gy, x_rows, width), BF16),
            pltpu.VMEM((x_rows, width), F32),
            pltpu.VMEM((n_low, own_rows, width), BF16),
            pltpu.VMEM((n_low, own_rows, width), BF16),
            pltpu.VMEM((width, units), BF16),
            pltpu.VMEM((units, width), BF16),
            dma((4,)),
            dma((n_gx,)),
            dma((n_gx,)),
            dma((2, 2, PIECES, n_gy // 2 + 1)),
            dma((2, 2, PIECES, n_gy // 2 + 1)),
            dma((CHUNKS, 2)),
            dma((CHUNKS, 2)),
            dma((CHUNKS, 4)),
            dma((CHUNKS, 4)),
            dma((CHUNKS, N_X)),
            dma((CHUNKS, N_X)),
            dma((n_gy,)),
            dma((n_gy,)),
            dma((n_gx // N_X,)),
            dma((n_gx // N_X,)),
        ],
        compiler_params=pltpu.CompilerParams(
            collective_id=0, has_side_effects=True, vmem_limit_bytes=VMEM_LIMIT
        ),
    )(tokens, w_up, w_down, cotangent)
    return pl.pallas_call(
        hand_over,
        out_shape=tuple(jax.ShapeDtypeStruct(a.shape, a.dtype) for a in results),
        in_specs=[pl.BlockSpec(memory_space=pltpu.VMEM)] * 3,
        out_specs=(pl.BlockSpec(memory_space=pltpu.VMEM),) * 3,
        compiler_params=pltpu.CompilerParams(vmem_limit_bytes=VMEM_LIMIT),
    )(*results)


def solution(mesh):
    sizes = tuple(mesh.shape[axis] for axis in ("gx", "gy", "gz"))
    placed = (
        P(("gx", "gy"), "gz"),
        P("gz", ("gx", "gy")),
        P(("gx", "gy"), "gz"),
        P(("gx", "gy"), "gz"),
    )
    return jax.shard_map(
        functools.partial(on_device, sizes),
        mesh=mesh,
        in_specs=placed,
        out_specs=(P(("gx", "gy"), "gz"), P("gz", ("gx", "gy")), P(("gx", "gy"), "gz")),
        check_vma=False,
    )
```

time: 100 us -> 93.5 us (0.935); the launches traced: 99.5 us -> 91.8 us
  local copies, waits for them, and re-layouts: 5.73 us -> 0 us
  Pallas kernels: 93.1 us -> 91.2 us
    unnamed x11 -> x0, local copies, waits for them, and re-layouts: 5.73 us -> none
    pallas_call x1, Pallas kernels: 93.1 us -> 88.9 us  [on_device(): pl.pallas_call(functools.partial(kernel, sizes), out_shape=(jax.ShapeDtyp...]
    pallas_call x0 -> x1, Pallas kernels: none -> 2.33 us  [on_device(): pl.pallas_call(hand_over, out_shape=tuple((jax.ShapeDtypeStruct(a.shape,...]
where the time goes in v3:
time: 93.5 us; the launch traced here: 91.8 us
  Pallas kernels  91.2 us (98%)
    pallas_call x1, Pallas kernels, on_device(): pl.pallas_call(functools.partial(kernel, sizes), out_shape=(jax.ShapeDtyp...  88.9 us
    pallas_call x1, Pallas kernels, on_device(): pl.pallas_call(hand_over, out_shape=tuple((jax.ShapeDtypeStruct(a.shape,...  2.33 us

profile of v3, /device:TPU:1, one launch (start us, length us, event | category | flops | bytes accessed | tf_op | source)
XLA Modules:
  0.0 91.8 jit_solution(10439595798647976425)
XLA Ops:
  0.6 88.9 %shard_map.67 = (f32[3,768]{1,0:T(4,128)}, bf16[768,384]{1,0:T(8,128)(2,1)}, bf16[384,768]{1,0:T(8,128)(2,1)}) custom-call(bf16[3,768]{1,0:T(4,128)(2,1)} %tokens_ref.1, bf16[768,384]{1,0:T(8,128)(2,1)} %w_up_ref.1, bf16[384,768]{1,0:T(8,128)(2,1)} %w_down_ref.1, bf16[3,768]{1,0:T(4,128)(2,1)} %cot_ref.1), custom_call_target="tpu_custom_call" | custom-call | tf_op jit(solution)/shard_map/pallas_call | solution.py:301
  89.5 2.3 %shard_map.68 = (f32[3,768]{1,0:T(4,128)}, bf16[768,384]{1,0:T(8,128)(2,1)}, bf16[384,768]{1,0:T(8,128)(2,1)}) custom-call(f32[3,768]{1,0:T(4,128)} %get-tuple-element.6.refs_0_, bf16[768,384]{1,0:T(8,128)(2,1)} %get-tuple-element.7.refs_1_, bf16[384,768]{1,0:T(8,128)(2,1)} %get-tuple-element.8.refs_2_), custom_call_target="tpu_custom_call" | custom-call | tf_op jit(solution)/shard_map/pallas_call | solution.py:356

commit v4 on v3

--- a/solution.py
+++ b/solution.py
@@ -44,9 +44,9 @@
     sizes,
     tokens_ref, w_up_ref, w_down_ref, cot_ref,
     grad_in_ref, grad_up_ref, grad_down_ref,
-    near, rows, wide, up, down, part, other, act,
+    near, far, rows, wide, up, down, up_t, down_t, part, other, act,
     pair_sum, pair_out, pair_in, back, x_out, x_in, back_out, back_in, own_sum, last_out, last_in, grad_up, grad_down,
-    local_sem, near_send, near_recv, y_send, y_recv, core_send, core_recv,
+    local_sem, near_send, near_recv, far_send, far_recv, y_send, y_recv, core_send, core_recv,
     z_send, z_recv, x_send, x_recv, back_send, back_recv, last_send, last_recv,
 ):
     n_gx, n_gy, n_gz = sizes
@@ -105,6 +105,11 @@
 
     for j in range(1, n_gx):
         send(near.at[0], near.at[j], near_send.at[j], near_recv.at[j], at_gx(j))
+    send(near.at[0], far.at[0], far_send.at[0], far_recv.at[0], at_gy(n_gy // 2))
+    load_up.wait()
+    load_down.wait()
+    down_t[...] = down[...].T
+    up_t[...] = up[...].T
     for j in range(n_gx):
         if j:
             arrived(near.at[j], near_recv.at[j])
@@ -112,17 +117,38 @@
             wide[which, j * own_rows : (j + 1) * own_rows] = near[j, which].astype(F32)
     rows[:, :slot_rows] = wide[...].astype(BF16)
 
+    def far_low():
+        arrived(far.at[0], far_recv.at[0])
+        for j in range(1, n_low):
+            send(far.at[0], far.at[j], far_send.at[j], far_recv.at[j], at_gx(j))
+
+    def far_x():
+        for j in range(1, n_low):
+            arrived(far.at[j], far_recv.at[j])
+        for j in range(1, N_X):
+            group = pl.ds(j * n_low, n_low)
+            send(
+                far.at[pl.ds(0, n_low)], far.at[group],
+                far_send.at[n_low + j], far_recv.at[n_low + j], at_gx(j * n_low),
+            )
+
+    def far_rows():
+        for j in range(N_X):
+            if j:
+                arrived(far.at[pl.ds(j * n_low, n_low)], far_recv.at[n_low + j])
+            for k in range(j * n_low, (j + 1) * n_low):
+                for which in range(2):
+                    wide[which, k * own_rows : (k + 1) * own_rows] = far[k, which].astype(F32)
+        first = slot_of(half) * slot_rows
+        rows[:, first : first + slot_rows] = wide[...].astype(BF16)
+
     half = n_gy // 2
     piece = slot_rows // PIECES
 
     def hop(step, which, at, way):
-        offset = step if way == 0 or step == half else -step
-        before = step - 1 if way == 0 else 1 - step
-        src, dst = (slot_of(o) * slot_rows + at * piece for o in (before, offset))
+        offsets = (step - 1, step) if way == 0 else (1 - step, -step)
+        src, dst = (slot_of(o) * slot_rows + at * piece for o in offsets)
         return rows.at[which, src : src + piece], rows.at[which, dst : dst + piece]
-
-    def travels(step, which, way):
-        return step < half or which == way
 
     def ring(step, which, at, way):
         src, dst = hop(step, which, at, way)
@@ -133,9 +159,9 @@
 
     def pass_on(step):
         for which, at, way in order:
-            if step and travels(step, which, way):
+            if step:
                 arrived(hop(step, which, at, way)[1], y_recv.at[way, which, at, step])
-            if step < half and travels(step + 1, which, way):
+            if step < half - 1:
                 ring(step + 1, which, at, way)
 
     def chunk(c):
@@ -145,7 +171,7 @@
         for which, value in enumerate(
             (
                 jnp.dot(rows[0, chunk(c)], up[...], preferred_element_type=F32),
-                dot_nt(rows[1, chunk(c)], down[...]),
+                jnp.dot(rows[1, chunk(c)], down_t[...], preferred_element_type=F32),
             )
         ):
             part[c, :, which] = value.reshape(n_gz, chunk_rows // n_gz, value.shape[1])
@@ -153,41 +179,61 @@
         send(theirs, other.at[c], core_send.at[c, 0], core_recv.at[c, 0], other_core)
 
     towards = 1 - 2 * (hi % 2)
-
-    def pair_send(c, step, which):
-        pair_out[c, step, which] = pair_sum[c, which].astype(BF16)
-        to = towards if (step + which) % 2 == 0 else -towards
-        send(
-            pair_out.at[c, step, which], pair_in.at[c, step, which],
-            z_send.at[c, 2 * step + which], z_recv.at[c, 2 * step + which], at_hi(to),
-        )
+    partner = (at_hi(towards), at_hi(-towards))
+    kept = ((hi // 2 + hi % 2) % 2, 2 + hi // 2)
+    given = (1 - kept[0], 5 - kept[1])
+
+    def chip_sum(c, tile):
+        return part[c, core * n_hi + tile] + other[c, tile]
+
+    def pair_send(c, step, which, to):
+        at = (c, step, which)
+        send(pair_out.at[at], pair_in.at[at], z_send.at[at], z_recv.at[at], partner[to])
 
     def pair_add(c, step, which):
-        arrived(pair_in.at[c, step, which], z_recv.at[c, 2 * step + which])
-        pair_sum[c, which] += pair_in[c, step, which].astype(F32)
+        at = (c, step, which)
+        arrived(pair_in.at[at], z_recv.at[at])
+        pair_sum[c, which] += pair_in[at].astype(F32)
+
+    def tile_of(c, tile, of=core):
+        return act.at[c, of * n_hi + tile]
+
+    def to_core(c, tile, at):
+        send(tile_of(c, tile), tile_of(c, tile), core_send.at[c, at], core_recv.at[c, at], other_core)
 
     def e1(c):
         arrived(other.at[c], core_recv.at[c, 0])
         for which in range(2):
-            pair_sum[c, which] = part[c, pl.ds(core * n_hi, n_hi), which] + other[c, :, which]
-            pair_send(c, 0, which)
+            pair_out[c, 0, which] = chip_sum(c, given[which]).astype(BF16)
+            pair_send(c, 0, which, which)
+        for which in range(2):
+            pair_sum[c, which] = chip_sum(c, kept[which])
 
     def e2(c):
         for which in range(2):
             pair_add(c, 0, which)
-            pair_send(c, 1, which)
+            pair_out[c, 1, which] = pair_sum[c, which].astype(BF16)
+            pair_send(c, 1, which, 1 - which)
 
     def e3(c):
         for which in range(2):
             pair_add(c, 1, which)
-        hidden, pre_grad = activate(pair_sum[c, 0], pair_sum[c, 1])
-        act[c, pl.ds(core * n_hi, n_hi), 0] = hidden
-        act[c, pl.ds(core * n_hi, n_hi), 1] = pre_grad
-        mine_all = act.at[c, pl.ds(core * n_hi, n_hi)]
-        send(mine_all, mine_all, core_send.at[c, 1], core_recv.at[c, 1], other_core)
+            hidden, pre_grad = activate(pair_sum[c, which, 0], pair_sum[c, which, 1])
+            act[c, core * n_hi + kept[which], 0] = hidden
+            act[c, core * n_hi + kept[which], 1] = pre_grad
+            tile = tile_of(c, kept[which])
+            send(tile, tile, z_send.at[c, 2, which], z_recv.at[c, 2, which], partner[which])
+            to_core(c, kept[which], 1 + which)
+
+    def e4(c):
+        for which in range(2):
+            arrived(tile_of(c, given[which]), z_recv.at[c, 2, which])
+            to_core(c, given[which], 3 + which)
 
     def e6(c):
-        arrived(act.at[c, pl.ds((1 - core) * n_hi, n_hi)], core_recv.at[c, 1])
+        for which in range(2):
+            arrived(tile_of(c, kept[which], 1 - core), core_recv.at[c, 1 + which])
+            arrived(tile_of(c, given[which], 1 - core), core_recv.at[c, 3 + which])
 
     def whole(c, which):
         return act[c, :, which].reshape(chunk_rows, act.shape[-1])
@@ -204,7 +250,7 @@
 
     def backward(c):
         first = c * chunk_rows
-        back[first : first + chunk_rows] = dot_nt(whole(c, 1), up[...])
+        back[first : first + chunk_rows] = jnp.dot(whole(c, 1), up_t[...], preferred_element_type=F32)
         done = sorted(finished(c))
         for j in range(1, N_X):
             for i, at in enumerate(done):
@@ -228,16 +274,29 @@
                 back_out[at] = total.astype(BF16)
                 send(back_out.at[at], back_in.at[at], back_send.at[at], back_recv.at[at], at_gy(slots[at]))
 
+    stores = (
+        pltpu.make_async_copy(grad_up, grad_up_ref, local_sem.at[0]),
+        pltpu.make_async_copy(grad_down, grad_down_ref, local_sem.at[1]),
+    )
+
+    def weights():
+        hidden = jnp.concatenate([whole(c, 0) for c in range(CHUNKS)])
+        pre_grad = jnp.concatenate([whole(c, 1) for c in range(CHUNKS)])
+        grad_up[...] = dot_tn(rows[0], pre_grad).astype(BF16)
+        stores[0].start()
+        grad_down[...] = dot_tn(hidden, rows[1]).astype(BF16)
+        stores[1].start()
+
     pass_on(0)
-    load_up.wait()
-    load_down.wait()
+    far_low()
     pass_on(1)
+    far_x()
     forward(0)
     pass_on(2)
     e1(0)
+    far_rows()
     pass_on(3)
     forward(1)
-    pass_on(4)
     e1(1)
     forward(2)
     e2(0)
@@ -245,26 +304,21 @@
     e2(1)
     e3(0)
     e2(2)
+    e3(1)
+    e4(0)
+    e3(2)
     e6(0)
     backward(0)
-    e3(1)
+    e4(1)
     e6(1)
     backward(1)
-    e3(2)
     sum_x(0)
+    e4(2)
     e6(2)
     backward(2)
     sum_x(1)
     sum_x(2)
-
-    hidden = jnp.concatenate([whole(c, 0) for c in range(CHUNKS)])
-    pre_grad = jnp.concatenate([whole(c, 1) for c in range(CHUNKS)])
-    grad_up[...] = dot_tn(rows[0], pre_grad).astype(BF16)
-    store_up = pltpu.make_async_copy(grad_up, grad_up_ref, local_sem.at[0])
-    store_up.start()
-    grad_down[...] = dot_tn(hidden, rows[1]).astype(BF16)
-    store_down = pltpu.make_async_copy(grad_down, grad_down_ref, local_sem.at[1])
-    store_down.start()
+    weights()
 
     for at in range(1, n_gy):
         arrived(back_in.at[at], back_recv.at[at])
@@ -277,15 +331,29 @@
         arrived(last_in.at[j], last_recv.at[j])
         result += last_in[j].astype(F32)
     grad_in_ref[...] = result
-    store_up.wait()
-    store_down.wait()
+    for store in stores:
+        store.wait()
     for copy in sent:
         copy.wait_send()
 
 
 def hand_over(*refs):
-    for src, dst in zip(refs[:3], refs[3:]):
-        dst[...] = src[...]
+    buffers, (loaded, stored) = refs[6:9], refs[9:]
+    loads, stores = [], []
+    for src, held, dst in zip(refs[:3], buffers, refs[3:6]):
+        parts = 4 if src.shape[0] % 64 == 0 else 1
+        size = src.shape[0] // parts
+        for p in range(parts):
+            part, n = pl.ds(p * size, size), len(loads)
+            loads.append(pltpu.make_async_copy(src.at[part], held.at[part], loaded.at[n]))
+            stores.append(pltpu.make_async_copy(held.at[part], dst.at[part], stored.at[n]))
+    for load in loads:
+        load.start()
+    for load, store in zip(loads, stores):
+        load.wait()
+        store.start()
+    for store in stores:
+        store.wait()
 
 
 def on_device(sizes, tokens, w_up, w_down, cotangent):
@@ -313,16 +381,19 @@
         ),
         scratch_shapes=[
             pltpu.VMEM((n_gx, 2, own_rows, width), BF16),
+            pltpu.VMEM((n_gx, 2, own_rows, width), BF16),
             pltpu.VMEM((2, total, width), BF16),
             pltpu.VMEM((2, slot_rows, width), F32),
             pltpu.VMEM((width, units), BF16),
             pltpu.VMEM((units, width), BF16),
+            pltpu.VMEM((units, width), BF16),
+            pltpu.VMEM((width, units), BF16),
             pltpu.VMEM((CHUNKS, n_gz, 2, r, units), F32),
             pltpu.VMEM((CHUNKS, n_hi, 2, r, units), F32),
             pltpu.VMEM((CHUNKS, n_gz, 2, r, units), BF16),
-            pltpu.VMEM((CHUNKS, 2, n_hi, r, units), F32),
-            pltpu.VMEM((CHUNKS, 2, 2, n_hi, r, units), BF16),
-            pltpu.VMEM((CHUNKS, 2, 2, n_hi, r, units), BF16),
+            pltpu.VMEM((CHUNKS, 2, 2, r, units), F32),
+            pltpu.VMEM((CHUNKS, 2, 2, 2, r, units), BF16),
+            pltpu.VMEM((CHUNKS, 2, 2, 2, r, units), BF16),
             pltpu.VMEM((total, width), F32),
             pltpu.VMEM((CHUNKS, N_X, n_gy // 2, x_rows, width), BF16),
             pltpu.VMEM((CHUNKS, N_X, n_gy // 2, x_rows, width), BF16),
@@ -336,12 +407,14 @@
             dma((4,)),
             dma((n_gx,)),
             dma((n_gx,)),
+            dma((n_low + N_X,)),
+            dma((n_low + N_X,)),
             dma((2, 2, PIECES, n_gy // 2 + 1)),
             dma((2, 2, PIECES, n_gy // 2 + 1)),
-            dma((CHUNKS, 2)),
-            dma((CHUNKS, 2)),
-            dma((CHUNKS, 4)),
-            dma((CHUNKS, 4)),
+            dma((CHUNKS, 5)),
+            dma((CHUNKS, 5)),
+            dma((CHUNKS, 3, 2)),
+            dma((CHUNKS, 3, 2)),
             dma((CHUNKS, N_X)),
             dma((CHUNKS, N_X)),
             dma((n_gy,)),
@@ -356,8 +429,9 @@
     return pl.pallas_call(
         hand_over,
         out_shape=tuple(jax.ShapeDtypeStruct(a.shape, a.dtype) for a in results),
-        in_specs=[pl.BlockSpec(memory_space=pltpu.VMEM)] * 3,
-        out_specs=(pl.BlockSpec(memory_space=pltpu.VMEM),) * 3,
+        in_specs=[pl.BlockSpec(memory_space=pl.ANY)] * 3,
+        out_specs=(pl.BlockSpec(memory_space=pl.ANY),) * 3,
+        scratch_shapes=[pltpu.VMEM(a.shape, a.dtype) for a in results] + [dma((9,)), dma((9,))],
         compiler_params=pltpu.CompilerParams(vmem_limit_bytes=VMEM_LIMIT),
     )(*results)
 

time: 93.5 us -> 90.7 us (0.970); the launches traced: 91.8 us -> 90 us
  Pallas kernels: 91.2 us -> 89.4 us
    pallas_call x1, Pallas kernels: 88.9 us -> 87.2 us  [on_device(): pl.pallas_call(functools.partial(kernel, sizes), out_shape=(jax.ShapeDtyp...]
where the time goes in v4:
time: 90.7 us; the launch traced here: 90 us
  Pallas kernels  89.4 us (99%)
    pallas_call x1, Pallas kernels, on_device(): pl.pallas_call(functools.partial(kernel, sizes), out_shape=(jax.ShapeDtyp...  87.2 us
    pallas_call x1, Pallas kernels, on_device(): pl.pallas_call(hand_over, out_shape=tuple((jax.ShapeDtypeStruct(a.shape,...  2.18 us

profile of v4, /device:TPU:1, one launch (start us, length us, event | category | flops | bytes accessed | tf_op | source)
XLA Modules:
  0.0 90.0 jit_solution(8263845599830355568)
XLA Ops:
  0.6 87.2 %shard_map.67 = (f32[3,768]{1,0:T(4,128)}, bf16[768,384]{1,0:T(8,128)(2,1)}, bf16[384,768]{1,0:T(8,128)(2,1)}) custom-call(bf16[3,768]{1,0:T(4,128)(2,1)} %tokens_ref.1, bf16[768,384]{1,0:T(8,128)(2,1)} %w_up_ref.1, bf16[384,768]{1,0:T(8,128)(2,1)} %w_down_ref.1, bf16[3,768]{1,0:T(4,128)(2,1)} %cot_ref.1), custom_call_target="tpu_custom_call" | custom-call | tf_op jit(solution)/shard_map/pallas_call | solution.py:369
  87.8 2.2 %shard_map.68 = (f32[3,768]{1,0:T(4,128)}, bf16[768,384]{1,0:T(8,128)(2,1)}, bf16[384,768]{1,0:T(8,128)(2,1)}) custom-call(f32[3,768]{1,0:T(4,128)} %get-tuple-element.6.refs_0_, bf16[768,384]{1,0:T(8,128)(2,1)} %get-tuple-element.7.refs_1_, bf16[384,768]{1,0:T(8,128)(2,1)} %get-tuple-element.8.refs_2_), custom_call_target="tpu_custom_call" | custom-call | tf_op jit(solution)/shard_map/pallas_call | solution.py:429

commit v5 on v4

--- a/solution.py
+++ b/solution.py
@@ -14,6 +14,8 @@
 BF16, F32 = jnp.bfloat16, jnp.float32
 CHUNKS = 3
 PIECES = 3
+FAR = (3, -3, 4)
+STEPS = 2
 VMEM_LIMIT = 63 * 1024 * 1024
 N_X = 4
 
@@ -105,7 +107,8 @@
 
     for j in range(1, n_gx):
         send(near.at[0], near.at[j], near_send.at[j], near_recv.at[j], at_gx(j))
-    send(near.at[0], far.at[0], far_send.at[0], far_recv.at[0], at_gy(n_gy // 2))
+    for n, offset in enumerate(FAR):
+        send(near.at[0], far.at[n, 0], far_send.at[n], far_recv.at[n], at_gy(-offset))
     load_up.wait()
     load_down.wait()
     down_t[...] = down[...].T
@@ -117,30 +120,33 @@
             wide[which, j * own_rows : (j + 1) * own_rows] = near[j, which].astype(F32)
     rows[:, :slot_rows] = wide[...].astype(BF16)
 
+    n_far = len(FAR)
+
     def far_low():
-        arrived(far.at[0], far_recv.at[0])
+        for n in range(n_far):
+            arrived(far.at[n, 0], far_recv.at[n])
         for j in range(1, n_low):
-            send(far.at[0], far.at[j], far_send.at[j], far_recv.at[j], at_gx(j))
+            send(far.at[:, 0], far.at[:, j], far_send.at[n_far + j], far_recv.at[n_far + j], at_gx(j))
 
     def far_x():
         for j in range(1, n_low):
-            arrived(far.at[j], far_recv.at[j])
+            arrived(far.at[:, j], far_recv.at[n_far + j])
         for j in range(1, N_X):
-            group = pl.ds(j * n_low, n_low)
+            at = n_far + n_low + j
             send(
-                far.at[pl.ds(0, n_low)], far.at[group],
-                far_send.at[n_low + j], far_recv.at[n_low + j], at_gx(j * n_low),
+                far.at[:, pl.ds(0, n_low)], far.at[:, pl.ds(j * n_low, n_low)],
+                far_send.at[at], far_recv.at[at], at_gx(j * n_low),
             )
 
     def far_rows():
-        for j in range(N_X):
-            if j:
-                arrived(far.at[pl.ds(j * n_low, n_low)], far_recv.at[n_low + j])
-            for k in range(j * n_low, (j + 1) * n_low):
+        for j in range(1, N_X):
+            arrived(far.at[:, pl.ds(j * n_low, n_low)], far_recv.at[n_far + n_low + j])
+        for n, offset in enumerate(FAR):
+            for k in range(n_gx):
                 for which in range(2):
-                    wide[which, k * own_rows : (k + 1) * own_rows] = far[k, which].astype(F32)
-        first = slot_of(half) * slot_rows
-        rows[:, first : first + slot_rows] = wide[...].astype(BF16)
+                    wide[which, k * own_rows : (k + 1) * own_rows] = far[n, k, which].astype(F32)
+            first = slot_of(offset) * slot_rows
+            rows[:, first : first + slot_rows] = wide[...].astype(BF16)
 
     half = n_gy // 2
     piece = slot_rows // PIECES
@@ -161,7 +167,7 @@
         for which, at, way in order:
             if step:
                 arrived(hop(step, which, at, way)[1], y_recv.at[way, which, at, step])
-            if step < half - 1:
+            if step < STEPS:
                 ring(step + 1, which, at, way)
 
     def chunk(c):
@@ -295,7 +301,6 @@
     pass_on(2)
     e1(0)
     far_rows()
-    pass_on(3)
     forward(1)
     e1(1)
     forward(2)
@@ -317,8 +322,8 @@
     e6(2)
     backward(2)
     sum_x(1)
+    weights()
     sum_x(2)
-    weights()
 
     for at in range(1, n_gy):
         arrived(back_in.at[at], back_recv.at[at])
@@ -381,7 +386,7 @@
         ),
         scratch_shapes=[
             pltpu.VMEM((n_gx, 2, own_rows, width), BF16),
-            pltpu.VMEM((n_gx, 2, own_rows, width), BF16),
+            pltpu.VMEM((len(FAR), n_gx, 2, own_rows, width), BF16),
             pltpu.VMEM((2, total, width), BF16),
             pltpu.VMEM((2, slot_rows, width), F32),
             pltpu.VMEM((width, units), BF16),
@@ -407,8 +412,8 @@
             dma((4,)),
             dma((n_gx,)),
             dma((n_gx,)),
-            dma((n_low + N_X,)),
-            dma((n_low + N_X,)),
+            dma((len(FAR) + n_low + N_X,)),
+            dma((len(FAR) + n_low + N_X,)),
             dma((2, 2, PIECES, n_gy // 2 + 1)),
             dma((2, 2, PIECES, n_gy // 2 + 1)),
             dma((CHUNKS, 5)),

time: 90.7 us -> 88.5 us (0.976)
  Pallas kernels: 89.4 us -> 86.9 us
    pallas_call x1, Pallas kernels: 87.2 us -> 84.7 us  [on_device(): pl.pallas_call(functools.partial(kernel, sizes), out_shape=(jax.ShapeDtyp...]
where the time goes in v5:
time: 88.5 us; the launch traced here: 87.5 us
  Pallas kernels  86.9 us (98%)
    pallas_call x1, Pallas kernels, on_device(): pl.pallas_call(functools.partial(kernel, sizes), out_shape=(jax.ShapeDtyp...  84.7 us
    pallas_call x1, Pallas kernels, on_device(): pl.pallas_call(hand_over, out_shape=tuple((jax.ShapeDtypeStruct(a.shape,...  2.18 us

profile of v5, /device:TPU:1, one launch (start us, length us, event | category | flops | bytes accessed | tf_op | source)
XLA Modules:
  0.0 87.5 jit_solution(8918035143399829544)
XLA Ops:
  0.6 84.7 %shard_map.67 = (f32[3,768]{1,0:T(4,128)}, bf16[768,384]{1,0:T(8,128)(2,1)}, bf16[384,768]{1,0:T(8,128)(2,1)}) custom-call(bf16[3,768]{1,0:T(4,128)(2,1)} %tokens_ref.1, bf16[768,384]{1,0:T(8,128)(2,1)} %w_up_ref.1, bf16[384,768]{1,0:T(8,128)(2,1)} %w_down_ref.1, bf16[3,768]{1,0:T(4,128)(2,1)} %cot_ref.1), custom_call_target="tpu_custom_call" | custom-call | tf_op jit(solution)/shard_map/pallas_call | solution.py:374
  85.3 2.2 %shard_map.68 = (f32[3,768]{1,0:T(4,128)}, bf16[768,384]{1,0:T(8,128)(2,1)}, bf16[384,768]{1,0:T(8,128)(2,1)}) custom-call(f32[3,768]{1,0:T(4,128)} %get-tuple-element.6.refs_0_, bf16[768,384]{1,0:T(8,128)(2,1)} %get-tuple-element.7.refs_1_, bf16[384,768]{1,0:T(8,128)(2,1)} %get-tuple-element.8.refs_2_), custom_call_target="tpu_custom_call" | custom-call | tf_op jit(solution)/shard_map/pallas_call | solution.py:434

commit v6 on v5

--- a/solution.py
+++ b/solution.py
@@ -47,9 +47,9 @@
     tokens_ref, w_up_ref, w_down_ref, cot_ref,
     grad_in_ref, grad_up_ref, grad_down_ref,
     near, far, rows, wide, up, down, up_t, down_t, part, other, act,
-    pair_sum, pair_out, pair_in, back, x_out, x_in, back_out, back_in, own_sum, last_out, last_in, grad_up, grad_down,
+    pair_sum, pair_out, pair_in, back, x_out, x_in, own_sum, last_out, last_in, grad_up, grad_down,
     local_sem, near_send, near_recv, far_send, far_recv, y_send, y_recv, core_send, core_recv,
-    z_send, z_recv, x_send, x_recv, back_send, back_recv, last_send, last_recv,
+    z_send, z_recv, x_send, x_recv, last_send, last_recv,
 ):
     n_gx, n_gy, n_gz = sizes
     n_hi = n_gz // 2
@@ -274,11 +274,14 @@
             total = group(at, 0)
             for j in range(1, N_X):
                 total += x_in[c, j, i].astype(F32)
-            if at == 0:
-                own_sum[...] = total
-            else:
-                back_out[at] = total.astype(BF16)
-                send(back_out.at[at], back_in.at[at], back_send.at[at], back_recv.at[at], at_gy(slots[at]))
+            for k in range(n_low):
+                value = total[k * own_rows : (k + 1) * own_rows]
+                if at == 0 and k == 0:
+                    own_sum[...] = value
+                else:
+                    last_out[at, k] = value.astype(BF16)
+                    owner = at_x * n_low + (low + n_low - k) % n_low, (gy + n_gy + slots[at]) % n_gy, gz
+                    send(last_out.at[at, k], last_in.at[at, k], last_send.at[at, k], last_recv.at[at, k], owner)
 
     stores = (
         pltpu.make_async_copy(grad_up, grad_up_ref, local_sem.at[0]),
@@ -325,16 +328,12 @@
     weights()
     sum_x(2)
 
-    for at in range(1, n_gy):
-        arrived(back_in.at[at], back_recv.at[at])
-        own_sum[...] += back_in[at].astype(F32)
-    for j in range(1, n_low):
-        last_out[j] = own_sum[j * own_rows : (j + 1) * own_rows].astype(BF16)
-        send(last_out.at[j], last_in.at[j], last_send.at[j], last_recv.at[j], at_gx(n_low - j))
-    result = own_sum[:own_rows]
-    for j in range(1, n_low):
-        arrived(last_in.at[j], last_recv.at[j])
-        result += last_in[j].astype(F32)
+    result = own_sum[...]
+    for at in range(n_gy):
+        for k in range(n_low):
+            if at or k:
+                arrived(last_in.at[at, k], last_recv.at[at, k])
+                result += last_in[at, k].astype(F32)
     grad_in_ref[...] = result
     for store in stores:
         store.wait()
@@ -402,11 +401,9 @@
             pltpu.VMEM((total, width), F32),
             pltpu.VMEM((CHUNKS, N_X, n_gy // 2, x_rows, width), BF16),
             pltpu.VMEM((CHUNKS, N_X, n_gy // 2, x_rows, width), BF16),
-            pltpu.VMEM((n_gy, x_rows, width), BF16),
-            pltpu.VMEM((n_gy, x_rows, width), BF16),
-            pltpu.VMEM((x_rows, width), F32),
-            pltpu.VMEM((n_low, own_rows, width), BF16),
-            pltpu.VMEM((n_low, own_rows, width), BF16),
+            pltpu.VMEM((own_rows, width), F32),
+            pltpu.VMEM((n_gy, n_low, own_rows, width), BF16),
+            pltpu.VMEM((n_gy, n_low, own_rows, width), BF16),
             pltpu.VMEM((width, units), BF16),
             pltpu.VMEM((units, width), BF16),
             dma((4,)),
@@ -422,10 +419,8 @@
             dma((CHUNKS, 3, 2)),
             dma((CHUNKS, N_X)),
             dma((CHUNKS, N_X)),
-            dma((n_gy,)),
-            dma((n_gy,)),
-            dma((n_gx // N_X,)),
-            dma((n_gx // N_X,)),
+            dma((n_gy, n_gx // N_X)),
+            dma((n_gy, n_gx // N_X)),
         ],
         compiler_params=pltpu.CompilerParams(
             collective_id=0, has_side_effects=True, vmem_limit_bytes=VMEM_LIMIT

time: 88.5 us -> 85.9 us (0.971)
  Pallas kernels: 86.9 us -> 85 us
    pallas_call x1, Pallas kernels: 84.7 us -> 82.8 us  [on_device(): pl.pallas_call(functools.partial(kernel, sizes), out_shape=(jax.ShapeDtyp...]
where the time goes in v6:
time: 85.9 us; the launch traced here: 85.7 us
  Pallas kernels  85 us (99%)
    pallas_call x1, Pallas kernels, on_device(): pl.pallas_call(functools.partial(kernel, sizes), out_shape=(jax.ShapeDtyp...  82.8 us
    pallas_call x1, Pallas kernels, on_device(): pl.pallas_call(hand_over, out_shape=tuple((jax.ShapeDtypeStruct(a.shape,...  2.18 us

profile of v6, /device:TPU:1, one launch (start us, length us, event | category | flops | bytes accessed | tf_op | source)
XLA Modules:
  0.0 85.7 jit_solution(4555077860134057068)
XLA Ops:
  0.6 82.8 %shard_map.67 = (f32[3,768]{1,0:T(4,128)}, bf16[768,384]{1,0:T(8,128)(2,1)}, bf16[384,768]{1,0:T(8,128)(2,1)}) custom-call(bf16[3,768]{1,0:T(4,128)(2,1)} %tokens_ref.1, bf16[768,384]{1,0:T(8,128)(2,1)} %w_up_ref.1, bf16[384,768]{1,0:T(8,128)(2,1)} %w_down_ref.1, bf16[3,768]{1,0:T(4,128)(2,1)} %cot_ref.1), custom_call_target="tpu_custom_call" | custom-call | tf_op jit(solution)/shard_map/pallas_call | solution.py:373
  83.5 2.2 %shard_map.68 = (f32[3,768]{1,0:T(4,128)}, bf16[768,384]{1,0:T(8,128)(2,1)}, bf16[384,768]{1,0:T(8,128)(2,1)}) custom-call(f32[3,768]{1,0:T(4,128)} %get-tuple-element.6.refs_0_, bf16[768,384]{1,0:T(8,128)(2,1)} %get-tuple-element.7.refs_1_, bf16[384,768]{1,0:T(8,128)(2,1)} %get-tuple-element.8.refs_2_), custom_call_target="tpu_custom_call" | custom-call | tf_op jit(solution)/shard_map/pallas_call | solution.py:429
